TPU v7x, 32 devices: a whole 2x2x4 slice. The times are simulated.
32 devices in a mesh: sub: 8 (over z, x), blk: 4 (over y, core).
Axes of the slice: x: 2, y: 2, z: 4, core: 2. Of those that a mesh axis runs over, the one named last changes fastest.
Arguments:
- modes: bfloat16 [16, 2048, 256], P('sub'), may hold values from -0.1875 to 0.1875
- stiff_blocks: bfloat16 [16, 128, 128, 128], P('sub', 'blk'), may hold values from -6 to 6
- mass_blocks: bfloat16 [16, 128, 128, 128], P('sub', 'blk'), may hold values from -6 to 6
- row_index: int32 [16, 128], P('sub', 'blk'), may hold values from 0 to 15
- col_index: int32 [16, 128], P('sub', 'blk'), may hold values from 0 to 3
- live_blocks: int32 [16, 4], P('sub', 'blk'), may hold values from 1 to 32, as said below
- dof_list: int32 [16, 2048], P('sub'), may hold values from 0 to 3071
- parent_basis: bfloat16 [24576, 2048], P('sub', 'blk'), may hold values from -0.125 to 0.125
- level_scale: float32 [8, 2048], P(None, 'blk'), may hold values from 0.35 to 1.4
Outputs:
- ancestor_sum: bfloat16 [8, 2, 256, 2048], P('sub', None, None, 'blk')
Inputs may be any that keep to these rules, and one draw needn't show every extreme that they name: live_blocks reaches 32 in every draw.
All inputs are finite; a program needn't handle non-finite values.
Results may differ from a plain program's by a relative error of at most 0.0049.
Values may be sent and summed in bfloat16 or wider, within the bound.
A program may use at most 64 MiB of HBM per device.

v0:
```python
import jax
import jax.numpy as jnp
from jax import lax
from jax.sharding import PartitionSpec as P

COLB_DEV = 4


def passed_along(block, axis, distance):
    devices = range(lax.axis_size(axis))
    route = [(i - distance, i) for i in devices if i - distance in devices]
    return lax.ppermute(block, axis, route)


def leaf_coupling(picked, blocks, onehot):
    prod = jnp.einsum("lnkr,lnkc->lnrc", picked, blocks, preferred_element_type=jnp.float32)
    tiles = jnp.einsum("lnrc,lng->lrgc", prod, onehot, precision=lax.Precision.HIGHEST)
    return tiles.reshape(tiles.shape[0], tiles.shape[1], tiles.shape[2] * tiles.shape[3])


def per_device(
    modes,
    stiff_blocks,
    mass_blocks,
    row_index,
    col_index,
    live_blocks,
    dof_list,
    parent_basis,
    level_scale,
):
    leaf_count = modes.shape[0]
    block = stiff_blocks.shape[2]
    slots = stiff_blocks.shape[1]
    phi = modes.reshape(leaf_count, modes.shape[1] // block, block, modes.shape[2])
    picked = jax.vmap(lambda table, which: table[which])(phi, row_index)
    live = jnp.arange(slots, dtype=jnp.int32)[None, :] < live_blocks
    onehot = (
        (col_index[:, :, None] == jnp.arange(COLB_DEV, dtype=jnp.int32)[None, None, :])
        & live[:, :, None]
    ).astype(jnp.float32)
    coupling = jnp.stack(
        [leaf_coupling(picked, stiff_blocks, onehot), leaf_coupling(picked, mass_blocks, onehot)],
        axis=1,
    ).astype(jnp.bfloat16)
    rows = jax.vmap(lambda which: parent_basis[which])(dof_list)
    reduced = jnp.einsum(
        "lmrc,lcb->lmrb",
        lax.all_gather(coupling, "blk", axis=3, tiled=True),
        rows,
        preferred_element_type=jnp.float32,
    )
    node = level_scale[0][None, None, :] * (reduced[0] + reduced[1])
    levels = lax.axis_size("sub").bit_length() - 1
    stored = [node]
    for k in range(1, levels + 1):
        incoming = passed_along(node, "sub", -(1 << k - 1))
        node = level_scale[k][None, None, :] * (node + incoming)
        stored.append(node)
    position = lax.axis_index("sub")
    total = stored[levels]
    for k in range(levels, 0, -1):
        arriving = passed_along(total, "sub", 1 << k - 1)
        owner = position % (1 << k) == 0
        total = jnp.where(owner, total, arriving) + stored[k - 1]
    return total[None].astype(jnp.bfloat16)


def solution(mesh):
    in_specs = (
        P("sub", None, None),
        P("sub", "blk", None, None),
        P("sub", "blk", None, None),
        P("sub", "blk"),
        P("sub", "blk"),
        P("sub", "blk"),
        P("sub", None),
        P("sub", "blk"),
        P(None, "blk"),
    )
    out_specs = P("sub", None, None, "blk")
    return jax.shard_map(
        per_device, mesh=mesh, in_specs=in_specs, out_specs=out_specs, check_vma=False
    )
```

profile of v0, /device:TPU:0, one launch (start us, length us, event | category | flops | bytes accessed | tf_op | source)
XLA Modules:
  0.0 278.6 jit_solution(460433400344477147)
XLA Ops:
  8.2 4.4 %gather_fusion.1 = bf16[64,128,256]{2,1,0:T(8,128)(2,1)} fusion(bf16[2,16,128,256]{3,2,1,0:T(8,128)(2,1)} %bitcast.51, s32[64]{0:T(128)S(1)} %reshape.41), kind=kCustom, calls=%fused_computation.1 | custom fusion | bytes 8389120 | tf_op jit(solution)/shard_map/vmap()/gather | solution.py:36
  12.6 4.2 %fusion.29 = f32[2,32,256,128]{3,2,1,0:T(8,128)S(1)} fusion(bf16[2,32,128,256]{3,2,1,0:T(8,128)(2,1)} %bitcast.49, bf16[2,32,128,128]{3,2,1,0:T(8,128)(2,1)} %param.10), kind=kOutput, calls=%fused_computation.34 | convolution fusion | flops 536870912 | bytes 14680064 | tf_op jit(solution)/shard_map/lnkr,lnkc->lnrc/dot_general | solution.py:16
  16.8 8.4 %fusion.13 = bf16[2,256,4,128]{3,2,1,0:T(4,128)(2,1)} fusion(f32[2,32,256,128]{3,2,1,0:T(8,128)S(1)} %fusion.29, s32[2,32]{1,0:T(2,128)S(1)} %copy-done.5, pred[2,32]{1,0:T(4,128)(4,1)S(1)} %iota_compare_fusion.1), kind=kOutput, calls=%fused_computation.9 | convolution fusion | flops 100925952 | bytes 8913216 | tf_op jit(solution)/shard_map/lnrc,lng->lrgc/dot_general | solution.py:17
  25.2 2.0 stack_reshape.8
  27.2 4.2 %fusion.30 = f32[2,32,256,128]{3,2,1,0:T(8,128)S(1)} fusion(bf16[2,32,128,256]{3,2,1,0:T(8,128)(2,1)} %bitcast.50, bf16[2,32,128,128]{3,2,1,0:T(8,128)(2,1)} %param.11), kind=kOutput, calls=%fused_computation.35 | convolution fusion | flops 536870912 | bytes 14680064 | tf_op jit(solution)/shard_map/lnkr,lnkc->lnrc/dot_general | solution.py:16
  31.4 8.6 %fusion.10 = bf16[2,256,4,128]{3,2,1,0:T(4,128)(2,1)} fusion(f32[2,32,256,128]{3,2,1,0:T(8,128)S(1)} %fusion.30, s32[2,32]{1,0:T(2,128)S(1)} %copy-done.5, pred[2,32]{1,0:T(4,128)(4,1)S(1)} %iota_compare_fusion.1), kind=kOutput, calls=%fused_computation.8 | convolution fusion | flops 100925952 | bytes 8913216 | tf_op jit(solution)/shard_map/lnrc,lng->lrgc/dot_general | solution.py:17
  39.9 2.1 stack_reshape.9
  42.0 2.4 pad_maximum_fusion
  44.4 17.4 %gather_fusion = bf16[4096,512]{1,0:T(8,128)(2,1)} fusion(bf16[3072,512]{1,0:T(8,128)(2,1)S(1)} %copy-done, s32[4096]{0:T(1024)S(1)} %broadcast_clamp_fusion), kind=kCustom, calls=%fused_computation | custom fusion | bytes 8404992 | tf_op jit(solution)/shard_map/vmap()/gather | solution.py:46
  61.9 19.8 %all-gather.2.cloned.1.call-done = bf16[2,2,256,2048]{3,2,1,0:T(8,128)(2,1)} async-done(((bf16[2,2,256,512]{3,2,1,0:T(8,128)(2,1)}), bf16[2,2,256,2048]{3,2,1,0:T(8,128)(2,1)}) %all-gather.2.cloned.1.call-update) | async-done | bytes 4194320 | tf_op jit(solution)/shard_map/all_gather | solution.py:49
  81.7 5.8 %fusion.31 = f32[2,2,256,512]{3,2,1,0:T(8,128)S(1)} fusion(bf16[2,2,256,2048]{3,2,1,0:T(8,128)(2,1)} %all-gather.2.cloned.1.call-done, bf16[2,2048,512,1]{2,1,3,0:T(8,128)(2,1)} %bitcast.52), kind=kOutput, calls=%fused_computation.36 | convolution fusion | flops 2147483648 | bytes 10485760 | tf_op jit(solution)/shard_map/lmrc,lcb->lmrb/dot_general | solution.py:47
  87.7 1.3 collective-permute-start
  89.0 25.9 %collective-permute-done = f32[2,256,512]{2,1,0:T(8,128)S(1)} collective-permute-done((f32[2,256,512]{2,1,0:T(8,128)S(1)}, f32[2,256,512]{2,1,0:T(8,128)S(1)}, u32[]{:S(2)}, u32[]{:S(2)}) %collective-permute-start) | collective-permute-done | bytes 1048608 | tf_op jit(solution)/shard_map/ppermute | solution.py:12
  116.6 25.1 %collective-permute-done.1 = f32[2,256,512]{2,1,0:T(8,128)S(1)} collective-permute-done((f32[2,256,512]{2,1,0:T(8,128)S(1)}, f32[2,256,512]{2,1,0:T(8,128)S(1)}, u32[]{:S(2)}, u32[]{:S(2)}) %collective-permute-start.1) | collective-permute-done | bytes 1048608 | tf_op jit(solution)/shard_map/ppermute | solution.py:12
  143.3 47.5 %collective-permute-done.2 = f32[2,256,512]{2,1,0:T(8,128)S(1)} collective-permute-done((f32[2,256,512]{2,1,0:T(8,128)S(1)}, f32[2,256,512]{2,1,0:T(8,128)S(1)}, u32[]{:S(2)}, u32[]{:S(2)}) %collective-permute-start.2) | collective-permute-done | bytes 1048608 | tf_op jit(solution)/shard_map/ppermute | solution.py:12
  192.1 2.4 collective-permute-start.3
  194.5 21.0 %collective-permute-done.3 = f32[2,256,512]{2,1,0:T(8,128)} collective-permute-done((f32[2,256,512]{2,1,0:T(8,128)}, f32[2,256,512]{2,1,0:T(8,128)}, u32[]{:S(2)}, u32[]{:S(2)}) %collective-permute-start.3) | collective-permute-done | bytes 1048608 | tf_op jit(solution)/shard_map/ppermute | solution.py:12
  215.5 2.9 %select_add_fusion.1 = f32[2,256,512]{2,1,0:T(8,128)} fusion(f32[2,256,512]{2,1,0:T(8,128)} %copy-done.3, f32[2,256,512]{2,1,0:T(8,128)} %add_multiply_fusion, f32[2,256,512]{2,1,0:T(8,128)} %collective-permute-done.3, pred[]{:T(512)S(6)} %eq.28), kind=kLoop, calls=%fused_computation.16 | loop fusion | flops 524288 | bytes 4194305 | tf_op jit(solution)/shard_map/add | solution.py:65
  218.4 2.3 collective-permute-start.4
  220.7 20.4 %collective-permute-done.4 = f32[2,256,512]{2,1,0:T(8,128)} collective-permute-done((f32[2,256,512]{2,1,0:T(8,128)}, f32[2,256,512]{2,1,0:T(8,128)}, u32[]{:S(2)}, u32[]{:S(2)}) %collective-permute-start.4) | collective-permute-done | bytes 1048608 | tf_op jit(solution)/shard_map/ppermute | solution.py:12
  241.1 2.9 %select_add_fusion = f32[2,256,512]{2,1,0:T(8,128)} fusion(f32[2,256,512]{2,1,0:T(8,128)} %copy-done.2, f32[2,256,512]{2,1,0:T(8,128)} %select_add_fusion.1, f32[2,256,512]{2,1,0:T(8,128)} %collective-permute-done.4, pred[]{:T(512)S(6)} %eq.27), kind=kLoop, calls=%fused_computation.15 | loop fusion | flops 524288 | bytes 4194305 | tf_op jit(solution)/shard_map/add | solution.py:65
  244.0 5.2 %collective-permute-start.5 = (f32[2,256,512]{2,1,0:T(8,128)}, f32[2,256,512]{2,1,0:T(8,128)}, u32[]{:S(2)}, u32[]{:S(2)}) collective-permute-start(f32[2,256,512]{2,1,0:T(8,128)} %select_add_fusion), channel_id=1, source_target_pairs={{0,4},{4,8},{8,12},{12,16},{16,20},{20,24},{24,28},{1,5},{5,9},{9,... | collective-permute-start | bytes 3145736 | tf_op jit(solution)/shard_map/ppermute | solution.py:12
  249.2 19.5 %collective-permute-done.5 = f32[2,256,512]{2,1,0:T(8,128)} collective-permute-done((f32[2,256,512]{2,1,0:T(8,128)}, f32[2,256,512]{2,1,0:T(8,128)}, u32[]{:S(2)}, u32[]{:S(2)}) %collective-permute-start.5) | collective-permute-done | bytes 1048608 | tf_op jit(solution)/shard_map/ppermute | solution.py:12
  268.6 3.1 %fusion.18 = bf16[1,2,256,512]{3,2,1,0:T(8,128)(2,1)} fusion(f32[2,256,512]{2,1,0:T(8,128)} %select_add_fusion, f32[2,256,512]{2,1,0:T(8,128)} %collective-permute-done.5, pred[]{:T(512)S(6)} %eq.26, f32[2,2,256,512]{3,2,1,0:T(8,128)} %copy-done.1, f32[512]{0:T(512)S(1)} %bitcast.58), kind=kLoop, calls=%fused_computation.20 | loop fusion | flops 1310720 | bytes 4720641 | tf_op jit(solution)/shard_map/convert_element_type | solution.py:66
  (29 shorter events, 6.4 us)
Async XLA Ops:
  6.5 37.9 %copy-start = (bf16[3072,512]{1,0:T(8,128)(2,1)S(1)}, bf16[3072,512]{1,0:T(8,128)(2,1)}, u32[]{:S(2)}) copy-start(bf16[3072,512]{1,0:T(8,128)(2,1)} %param.16) | copy-start | bytes 9437188
  6.5 75.2 %all-gather.2.cloned.1.call-start = ((), (), s32[]{:S(2)}) async-start(), calls=%async_computation | async-start | bytes 5242880 | tf_op jit(solution)/shard_map/all_gather | solution.py:49
  12.6 4.2 %copy-start.5 = (s32[2,32]{1,0:T(2,128)S(1)}, s32[2,32]{1,0:T(2,128)}, u32[]{:S(2)}) copy-start(s32[2,32]{1,0:T(2,128)} %param.13) | copy-start | bytes 772
  39.9 4.4 %copy-start.4 = (s32[2,2048]{1,0:T(2,128)S(1)}, s32[2,2048]{1,0:T(2,128)}, u32[]{:S(2)}) copy-start(s32[2,2048]{1,0:T(2,128)} %param.15) | copy-start | bytes 49156
  44.4 17.4 %copy-start.6 = (f32[8,512]{1,0:T(8,128)S(1)}, f32[8,512]{1,0:T(8,128)}, u32[]{:S(2)}) copy-start(f32[8,512]{1,0:T(8,128)} %param.17) | copy-start | bytes 49156
  87.5 54.5 %copy-start.1 = (f32[2,2,256,512]{3,2,1,0:T(8,128)}, f32[2,2,256,512]{3,2,1,0:T(8,128)S(1)}, u32[]{:S(2)}) copy-start(f32[2,2,256,512]{3,2,1,0:T(8,128)S(1)} %fusion.31) | copy-start | bytes 6291460
  87.7 27.2 %collective-permute-start = (f32[2,256,512]{2,1,0:T(8,128)S(1)}, f32[2,256,512]{2,1,0:T(8,128)S(1)}, u32[]{:S(2)}, u32[]{:S(2)}) collective-permute-start(f32[2,256,512]{2,1,0:T(8,128)S(1)} %fusion.17), channel_id=1, source_target_pairs={{4,0},{8,4},{12,8},{16,12},{20,16},{24,20},{28,24},{5,1},{9,5},{13... | collective-permute-start | bytes 3145736 | tf_op jit(solution)/shard_map/ppermute | solution.py:12
  115.3 28.0 %copy-start.2 = (f32[2,256,512]{2,1,0:T(8,128)}, f32[2,256,512]{2,1,0:T(8,128)S(1)}, u32[]{:S(2)}) copy-start(f32[2,256,512]{2,1,0:T(8,128)S(1)} %add_multiply_fusion.2) | copy-start | bytes 3145732
  115.3 26.4 %collective-permute-start.1 = (f32[2,256,512]{2,1,0:T(8,128)S(1)}, f32[2,256,512]{2,1,0:T(8,128)S(1)}, u32[]{:S(2)}, u32[]{:S(2)}) collective-permute-start(f32[2,256,512]{2,1,0:T(8,128)S(1)} %add_multiply_fusion.2), channel_id=1, source_target_pairs={{8,0},{12,4},{16,8},{20,12},{24,16},{28,20},{9,1},{13,5},{17,9},{2... | collective-permute-start | bytes 3145736 | tf_op jit(solution)/shard_map/ppermute | solution.py:12
  142.0 48.8 %copy-start.3 = (f32[2,256,512]{2,1,0:T(8,128)}, f32[2,256,512]{2,1,0:T(8,128)S(1)}, u32[]{:S(2)}) copy-start(f32[2,256,512]{2,1,0:T(8,128)S(1)} %add_multiply_fusion.1) | copy-start | bytes 3145732
  142.0 48.8 %collective-permute-start.2 = (f32[2,256,512]{2,1,0:T(8,128)S(1)}, f32[2,256,512]{2,1,0:T(8,128)S(1)}, u32[]{:S(2)}, u32[]{:S(2)}) collective-permute-start(f32[2,256,512]{2,1,0:T(8,128)S(1)} %add_multiply_fusion.1), channel_id=1, source_target_pairs={{16,0},{20,4},{24,8},{28,12},{17,1},{21,5},{25,9},{29,13},{18,2},{... | collective-permute-start | bytes 3145736 | tf_op jit(solution)/shard_map/ppermute | solution.py:12
  192.1 23.5 %collective-permute-start.3 = (f32[2,256,512]{2,1,0:T(8,128)}, f32[2,256,512]{2,1,0:T(8,128)}, u32[]{:S(2)}, u32[]{:S(2)}) collective-permute-start(f32[2,256,512]{2,1,0:T(8,128)} %add_multiply_fusion), channel_id=1, source_target_pairs={{0,16},{4,20},{8,24},{12,28},{1,17},{5,21},{9,25},{13,29},{2,18},{... | collective-permute-start | bytes 3145736 | tf_op jit(solution)/shard_map/ppermute | solution.py:12
  218.4 22.7 %collective-permute-start.4 = (f32[2,256,512]{2,1,0:T(8,128)}, f32[2,256,512]{2,1,0:T(8,128)}, u32[]{:S(2)}, u32[]{:S(2)}) collective-permute-start(f32[2,256,512]{2,1,0:T(8,128)} %select_add_fusion.1), channel_id=1, source_target_pairs={{0,8},{4,12},{8,16},{12,20},{16,24},{20,28},{1,9},{5,13},{9,17},{1... | collective-permute-start | bytes 3145736 | tf_op jit(solution)/shard_map/ppermute | solution.py:12
  244.0 24.6 %collective-permute-start.5 = (f32[2,256,512]{2,1,0:T(8,128)}, f32[2,256,512]{2,1,0:T(8,128)}, u32[]{:S(2)}, u32[]{:S(2)}) collective-permute-start(f32[2,256,512]{2,1,0:T(8,128)} %select_add_fusion), channel_id=1, source_target_pairs={{0,4},{4,8},{8,12},{12,16},{16,20},{20,24},{24,28},{1,5},{5,9},{9,... | collective-permute-start | bytes 3145736 | tf_op jit(solution)/shard_map/ppermute | solution.py:12
Sparse Core Ops, SparseCore 0:
  44.5 37.1 all-gather.1
where the time goes:
time: 282 us; the launch traced here: 279 us
  waiting for transfers between devices  179 us (63%)
  matrix products  31 us (11%)
  local copies, waits for them, and re-layouts  26 us (9%)
  other arithmetic  15 us (5%)
  starting transfers between devices  13.8 us (5%)
  between operations  13.6 us (5%)
    ppermute x6, waiting for transfers between devices, passed_along(): return lax.ppermute(block, axis, route)  159 us
    all_gather x1, waiting for transfers between devices, per_device(): lax.all_gather(coupling, 'blk', axis=3, tiled=True)  19.8 us
    gather x1, local copies, waits for them, and re-layouts, per_device(): rows = jax.vmap(lambda which: parent_basis[which])(dof_list)  17.4 us
    dot_general x2, matrix products, leaf_coupling(): jnp.einsum('lnrc,lng->lrgc', prod, onehot, precision=lax.Precision.HIGHEST)  16.9 us
    ppermute x6, starting transfers between devices, passed_along(): return lax.ppermute(block, axis, route)  13.8 us
    dot_general x2, matrix products, leaf_coupling(): jnp.einsum('lnkr,lnkc->lnrc', picked, blocks, preferred_element_type=jnp....  8.33 us
    add x2, other arithmetic, per_device(): total = jnp.where(owner, total, arriving) + stored[k - 1]  5.8 us
    dot_general x1, matrix products, per_device(): jnp.einsum('lmrc,lcb->lmrb', lax.all_gather(coupling, 'blk', axis=3, tile...  5.79 us
  transfers between devices with their start and end apart: 7, of which 7 were waited for; matrix products, arithmetic and copies ran while one was open for 6% of the time, Pallas kernels for 0%

commit v1 on v0

v1 whole, which is shorter than its diff:
```python
import functools

import jax
import jax.numpy as jnp
from jax import lax
from jax.experimental import pallas as pl
from jax.experimental.pallas import tpu as pltpu
from jax.sharding import PartitionSpec as P

COLB_DEV = 4
GROUP = 4
HALVES = 2
MESH = pl.DeviceIdType.MESH


def coupling_kernel(rows_ref, cols_ref, live_ref, modes_ref, stiff_ref, mass_ref, out_ref, phi_t, acc):
    leaf = pl.program_id(0)
    slots, block = stiff_ref.shape[1], stiff_ref.shape[2]
    rowb = modes_ref.shape[1] // block
    half = modes_ref.shape[2] // HALVES
    for r in range(rowb):
        phi_t[r] = modes_ref[0, r * block : (r + 1) * block, :].T
    acc[...] = jnp.zeros_like(acc)
    live = live_ref[leaf, 0]

    def step(g, carry):
        prods = []
        for u in range(GROUP):
            j = g * GROUP + u
            pair = jnp.concatenate([stiff_ref[0, j], mass_ref[0, j]], axis=1)
            prods.append(jnp.dot(phi_t[rows_ref[leaf, j]], pair, preferred_element_type=jnp.float32))
        for u in range(GROUP):
            j = g * GROUP + u
            col = jnp.where(j < live, cols_ref[leaf, j], COLB_DEV)
            acc[col] += prods[u]
        return carry

    lax.fori_loop(0, (live + GROUP - 1) // GROUP, step, 0)
    for c in range(COLB_DEV):
        for m in range(2):
            for h in range(HALVES):
                out_ref[m * HALVES + h, 0, :, c * block : (c + 1) * block] = acc[
                    c, h * half : (h + 1) * half, m * block : (m + 1) * block
                ].astype(out_ref.dtype)


def leaf_couplings(row_index, col_index, live_blocks, modes, stiff, mass):
    leaves, ni, nmodes = modes.shape
    slots, block = stiff.shape[1], stiff.shape[2]
    half = nmodes // HALVES
    return pl.pallas_call(
        coupling_kernel,
        out_shape=jax.ShapeDtypeStruct((2 * HALVES, leaves, half, COLB_DEV * block), jnp.bfloat16),
        grid_spec=pltpu.PrefetchScalarGridSpec(
            num_scalar_prefetch=3,
            grid=(leaves,),
            in_specs=[
                pl.BlockSpec((1, ni, nmodes), lambda l, *_: (l, 0, 0)),
                pl.BlockSpec((1, slots, block, block), lambda l, *_: (l, 0, 0, 0)),
                pl.BlockSpec((1, slots, block, block), lambda l, *_: (l, 0, 0, 0)),
            ],
            out_specs=pl.BlockSpec((2 * HALVES, 1, half, COLB_DEV * block), lambda l, *_: (0, l, 0, 0)),
            scratch_shapes=[
                pltpu.VMEM((ni // block, nmodes, block), jnp.bfloat16),
                pltpu.VMEM((COLB_DEV + 1, nmodes, 2 * block), jnp.float32),
            ],
        ),
        compiler_params=pltpu.CompilerParams(vmem_limit_bytes=40 << 20),
        name="leaf_couplings",
    )(row_index, col_index, live_blocks, modes, stiff, mass)


UNROLL = 32


def rows_kernel(dof_ref, basis_ref, out_ref, table, picked):
    step = pl.program_id(0)
    np_, cols = basis_ref.shape
    nb = cols // 128
    count = out_ref.shape[0]

    @pl.when(step == 0)
    def _():
        for c in range(nb):
            table[pl.ds(c, np_, nb), :] = basis_ref[:, c * 128 : (c + 1) * 128].astype(jnp.float32)

    def body(i, carry):
        for u in range(UNROLL):
            t = i * UNROLL + u
            which = dof_ref[step * count + t]
            picked[pl.ds(t * nb, nb), :] = table[pl.ds(which * nb, nb), :]
        return carry

    lax.fori_loop(0, count // UNROLL, body, 0)
    for c in range(nb):
        out_ref[:, c * 128 : (c + 1) * 128] = picked[pl.ds(c, count, nb), :].astype(out_ref.dtype)


def basis_rows(dof_list, basis):
    total = dof_list.shape[0] * dof_list.shape[1]
    np_, cols = basis.shape
    count = 512
    return pl.pallas_call(
        rows_kernel,
        out_shape=jax.ShapeDtypeStruct((total, cols), jnp.bfloat16),
        grid_spec=pltpu.PrefetchScalarGridSpec(
            num_scalar_prefetch=1,
            grid=(total // count,),
            in_specs=[pl.BlockSpec((np_, cols), lambda i, *_: (0, 0))],
            out_specs=pl.BlockSpec((count, cols), lambda i, *_: (i, 0)),
            scratch_shapes=[
                pltpu.VMEM((np_ * cols // 128, 128), jnp.float32),
                pltpu.VMEM((count * cols // 128, 128), jnp.float32),
            ],
        ),
        compiler_params=pltpu.CompilerParams(vmem_limit_bytes=40 << 20),
        name="basis_rows",
    )(dof_list.reshape(total), basis)


def flipped(index, bit):
    return index + (1 << bit) * (1 - 2 * ((index // (1 << bit)) % 2))


def merge_kernel(
    levels, c_ref, rows_hbm, scale_ref, out_ref,
    rows, got, node0, part, node, total, sends, merged, t_send, t_got,
    rows_sem, y_send, y_recv, core_send, core_recv, fwd_send, fwd_recv, lev_send, lev_recv, t_ssem, t_rsem,
):
    q, b = lax.axis_index("sub"), lax.axis_index("blk")
    chunks, leaves, depth, width = c_ref.shape
    rows_copy = pltpu.make_async_copy(rows_hbm, rows, rows_sem)
    rows_copy.start()
    near, far = (q, flipped(b, 0)), (q, flipped(b, 1))
    peers = [(flipped(q, k), b) for k in range(levels)]
    barrier = pltpu.get_barrier_semaphore()
    for peer in [near, far] + peers:
        pl.semaphore_signal(barrier, inc=1, device_id=peer, device_id_type=MESH)
    pl.semaphore_wait(barrier, 2 + levels)

    def remote(src, dst, ssem, rsem, peer):
        return pltpu.make_async_remote_copy(
            src_ref=src, dst_ref=dst, send_sem=ssem, recv_sem=rsem, device_id=peer, device_id_type=MESH
        )

    far_copies = [remote(c_ref.at[i], got.at[1, i], y_send.at[i], y_recv.at[i], far) for i in range(chunks)]
    near_copies = [remote(c_ref.at[i], got.at[0, i], core_send.at[i], core_recv.at[i], near) for i in range(chunks)]
    fwd_copies = [remote(got.at[1, i], got.at[2, i], fwd_send.at[i], fwd_recv.at[i], near) for i in range(chunks)]
    lev_copies = [
        [remote(sends.at[k, i], merged.at[k, i], lev_send.at[k, i], lev_recv.at[k, i], peers[k]) for i in range(chunks)]
        for k in range(levels)
    ]
    t_copies = [remote(t_send.at[i], t_got.at[i], t_ssem.at[i], t_rsem.at[i], peers[0]) for i in range(chunks)]
    for copy in far_copies + near_copies:
        copy.start()
    rows_copy.wait()

    def product(tile, which):
        res = None
        for leaf in range(leaves):
            start = pl.multiple_of((leaf * 4 + which) * width, width)
            one = jnp.dot(tile[leaf], rows[pl.ds(start, width), :], preferred_element_type=jnp.float32)
            res = one if res is None else res + one
        return res

    half = depth // 2
    own = q % 2
    for i in range(chunks):
        part[i] = product(c_ref.at[i], b)
    for i in range(chunks):
        near_copies[i].wait_recv()
        part[i] += product(got.at[0, i], near[1])

    def leaf_stage(i):
        far_copies[i].wait_recv()
        fwd_copies[i].start()
        part[i] += product(got.at[1, i], far[1])
        fwd_copies[i].wait_recv()
        res = scale_ref[0:1, :] * (part[i] + product(got.at[2, i], flipped(far[1], 0)))
        node0[i, 0] = res[:half]
        node0[i, 1] = res[half:]
        if levels:
            sends[0, i] = node0[i, 1 - own].astype(sends.dtype)
            lev_copies[0][i].start()

    def level_stage(k, i):
        lev_copies[k - 1][i].wait_recv()
        mine = node0[i, own] if k == 1 else node[i]
        value = scale_ref[k : k + 1, :] * (mine + merged[k - 1, i].astype(jnp.float32))
        node[i] = value
        summed = value if k == 1 else total[i] + value
        total[i] = summed
        if k < levels:
            sends[k, i] = value.astype(sends.dtype)
            lev_copies[k][i].start()
        else:
            t_send[i] = summed.astype(t_send.dtype)
            t_copies[i].start()
            out_ref[i, own] = (node0[i, own] + summed).astype(out_ref.dtype)

    def last_stage(i):
        t_copies[i].wait_recv()
        out_ref[i, 1 - own] = (node0[i, 1 - own] + t_got[i].astype(jnp.float32)).astype(out_ref.dtype)

    stages = [leaf_stage] + [functools.partial(level_stage, k) for k in range(1, levels + 1)] + [last_stage]
    for t in range(chunks + len(stages) - 1):
        for s, stage in enumerate(stages):
            if 0 <= t - s < chunks:
                stage(t - s)
    for copy in far_copies + near_copies + fwd_copies + [c for row in lev_copies for c in row] + t_copies:
        copy.wait_send()


def merged_tree(coupling, rows, level_scale, levels):
    chunks, leaves, depth, width = coupling.shape
    cols = rows.shape[1]
    half = depth // 2
    bf, f32 = jnp.bfloat16, jnp.float32
    dma = pltpu.SemaphoreType.DMA
    vmem = pl.BlockSpec(memory_space=pltpu.VMEM)
    return pl.pallas_call(
        functools.partial(merge_kernel, levels),
        out_shape=jax.ShapeDtypeStruct((chunks, 2, half, cols), bf),
        in_specs=[vmem, pl.BlockSpec(memory_space=pl.ANY), vmem],
        out_specs=vmem,
        scratch_shapes=[
            pltpu.VMEM(rows.shape, bf),
            pltpu.VMEM((3, chunks, leaves, depth, width), bf),
            pltpu.VMEM((chunks, 2, half, cols), f32),
            pltpu.VMEM((chunks, depth, cols), f32),
            pltpu.VMEM((chunks, half, cols), f32),
            pltpu.VMEM((chunks, half, cols), f32),
            pltpu.VMEM((levels, chunks, half, cols), bf),
            pltpu.VMEM((levels, chunks, half, cols), bf),
            pltpu.VMEM((chunks, half, cols), bf),
            pltpu.VMEM((chunks, half, cols), bf),
            dma,
            dma((chunks,)), dma((chunks,)), dma((chunks,)), dma((chunks,)), dma((chunks,)), dma((chunks,)),
            dma((levels, chunks)), dma((levels, chunks)), dma((chunks,)), dma((chunks,)),
        ],
        compiler_params=pltpu.CompilerParams(
            collective_id=0, has_side_effects=True, vmem_limit_bytes=40 << 20
        ),
        name="merged_tree",
    )(coupling, rows, level_scale)


def per_device(
    modes,
    stiff_blocks,
    mass_blocks,
    row_index,
    col_index,
    live_blocks,
    dof_list,
    parent_basis,
    level_scale,
):
    levels = lax.axis_size("sub").bit_length() - 1
    coupling = leaf_couplings(row_index, col_index, live_blocks, modes, stiff_blocks, mass_blocks)
    rows = basis_rows(dof_list, parent_basis)
    out = merged_tree(coupling, rows, level_scale, levels)
    return out.reshape(1, 2, modes.shape[2], parent_basis.shape[1])


def solution(mesh):
    in_specs = (
        P("sub", None, None),
        P("sub", "blk", None, None),
        P("sub", "blk", None, None),
        P("sub", "blk"),
        P("sub", "blk"),
        P("sub", "blk"),
        P("sub", None),
        P("sub", "blk"),
        P(None, "blk"),
    )
    out_specs = P("sub", None, None, "blk")
    return jax.shard_map(
        per_device, mesh=mesh, in_specs=in_specs, out_specs=out_specs, check_vma=False
    )
```

time: 282 us -> 69.2 us (0.25); the launches traced: 279 us -> 69.8 us
  waiting for transfers between devices: 179 us -> 0 us
  Pallas kernels: 0 us -> 61.4 us
  matrix products: 31 us -> 0 us
  local copies, waits for them, and re-layouts: 26 us -> 8.39 us
  other arithmetic: 15 us -> 0 us
  starting transfers between devices: 13.8 us -> 0 us
  between operations: 13.6 us -> 0.06 us
    ppermute x6 -> x0, waiting for transfers between devices: 159 us -> none  [passed_along(): return lax.ppermute(block, axis, route)]
    pallas_call x0 -> x3, Pallas kernels: none -> 61.4 us  [the longest x1 49.2 us: merged_tree(): pl.pallas_call(functools.partial(merge_kernel, levels), out_shape=jax.Sha...]
    dot_general x5 -> x0, matrix products: 31 us -> none  [the longest x2 16.9 us: leaf_coupling(): jnp.einsum('lnrc,lng->lrgc', prod, onehot, precision=lax.Precision.HIGHEST)]
    gather x3 -> x0, local copies, waits for them, and re-layouts: 21.9 us -> none  [the longest x1 17.4 us: per_device(): rows = jax.vmap(lambda which: parent_basis[which])(dof_list)]
    all_gather x1 -> x0, waiting for transfers between devices: 19.8 us -> none  [per_device(): lax.all_gather(coupling, 'blk', axis=3, tiled=True)]
    ppermute x6 -> x0, starting transfers between devices: 13.8 us -> none  [passed_along(): return lax.ppermute(block, axis, route)]
    unnamed x15 -> x17, local copies, waits for them, and re-layouts: 0.03 us -> 8.39 us
    add x2 -> x0, other arithmetic: 5.8 us -> none  [per_device(): total = jnp.where(owner, total, arriving) + stored[k - 1]]
  transfers between devices with their start and end apart: 7 -> 0, of which waited for: 7 -> 0; matrix products, arithmetic and copies ran while one was open for 6% -> 0% of each run, Pallas kernels for 0% -> 0%
where the time goes in v1:
time: 69.2 us; the launch traced here: 69.8 us
  Pallas kernels  61.4 us (89%)
  local copies, waits for them, and re-layouts  8.39 us (12%)
    pallas_call x1, Pallas kernels, merged_tree(): pl.pallas_call(functools.partial(merge_kernel, levels), out_shape=jax.Sha...  49.2 us
    pallas_call x1, Pallas kernels, basis_rows(): pl.pallas_call(rows_kernel, out_shape=jax.ShapeDtypeStruct((total, cols),...  8.69 us
    unnamed x17, local copies, waits for them, and re-layouts  8.39 us
    pallas_call x1, Pallas kernels, leaf_couplings(): pl.pallas_call(coupling_kernel, out_shape=jax.ShapeDtypeStruct((2 * HALVE...  3.45 us

profile of v1, /device:TPU:0, one launch (start us, length us, event | category | flops | bytes accessed | tf_op | source)
XLA Modules:
  0.0 69.8 jit_solution(8755417138776464996)
XLA Ops:
  0.0 0.7 %copy.10.live_ref = s32[2,1]{1,0:T(2,128)S(1)} copy(s32[2,1]{0,1:T(1,128)} %param.14) | data formatting | bytes 16 | tf_op args[5]
  0.7 0.7 %copy.11 = s32[1,16,2,128]{3,1,2,0:T(8,128)S(1)} copy(s32[1,16,2,128]{3,2,1,0:T(2,128)} %bitcast.5) | data formatting | bytes 32768
  1.5 0.0 copy-start.1
  1.5 1.6 %copy-done.1 = bf16[2,2048,256]{2,1,0:T(8,128)(2,1)S(1)} copy-done((bf16[2,2048,256]{2,1,0:T(8,128)(2,1)S(1)}, bf16[2,2048,256]{2,1,0:T(8,128)(2,1)}, u32[]{:S(2)}) %copy-start.1) | copy-done | bytes 2097176
  3.1 0.0 copy-start.2
  3.1 1.6 %copy-done.2 = bf16[2,32,128,128]{3,2,1,0:T(8,128)(2,1)S(1)} copy-done((bf16[2,32,128,128]{3,2,1,0:T(8,128)(2,1)S(1)}, bf16[2,32,128,128]{3,2,1,0:T(8,128)(2,1)}, u32[]{:S(2)}) %copy-start.2) | copy-done | bytes 2097176
  4.6 0.0 copy-start.3
  4.6 1.6 %copy-done.3 = bf16[2,32,128,128]{3,2,1,0:T(8,128)(2,1)S(1)} copy-done((bf16[2,32,128,128]{3,2,1,0:T(8,128)(2,1)S(1)}, bf16[2,32,128,128]{3,2,1,0:T(8,128)(2,1)}, u32[]{:S(2)}) %copy-start.3) | copy-done | bytes 2097176
  6.2 0.0 copy-start.5
  6.2 0.7 copy-done.5
  6.9 0.0 copy-start.6
  6.9 0.7 copy-done.6
  7.6 0.0 copy-start
  7.6 3.4 %leaf_couplings.1.c_ref = bf16[4,2,128,512]{3,2,1,0:T(8,128)(2,1)S(1)} custom-call(s32[2,32]{1,0:T(2,128)S(1)} %copy-done.5, s32[2,32]{1,0:T(2,128)S(1)} %copy-done.6, s32[2,1]{1,0:T(2,128)S(1)} %copy.10.live_ref, bf16[2,2048,256]{2,1,0:T(8,128)(2,1)S(1)} %copy-done.1, bf16[2,32,128,128]{3,2,1,0:T(8,128)(2,1)S(1)} %copy-done.2, ...), custom_call_target="tpu_custom_call" | custom-call | tf_op jit(solution)/shard_map/leaf_couplings/pallas_call | solution.py:51
  11.1 0.0 copy-done
  11.1 0.0 copy-start.4
  11.1 8.7 %basis_rows.1.rows_hbm = bf16[4096,512]{1,0:T(8,128)(2,1)S(1)} custom-call(s32[4096]{0:T(1024)S(1)} %bitcast.4, bf16[3072,512]{1,0:T(8,128)(2,1)S(1)} %copy-done), custom_call_target="tpu_custom_call" | custom-call | tf_op jit(solution)/shard_map/basis_rows/pallas_call | solution.py:103
  19.8 0.0 copy-done.4
  19.8 49.2 %merged_tree.1 = bf16[4,2,64,512]{3,2,1,0:T(8,128)(2,1)S(1)} custom-call(bf16[4,2,128,512]{3,2,1,0:T(8,128)(2,1)S(1)} %leaf_couplings.1.c_ref, bf16[4096,512]{1,0:T(8,128)(2,1)S(1)} %basis_rows.1.rows_hbm, f32[8,512]{1,0:T(8,128)S(1)} %copy-done.4), custom_call_target="tpu_custom_call" | custom-call | tf_op jit(solution)/shard_map/merged_tree/pallas_call | solution.py:221
  69.0 0.8 %copy.13 = bf16[1,2,256,512]{3,2,1,0:T(8,128)(2,1)} copy(bf16[1,2,256,512]{3,2,1,0:T(8,128)(2,1)S(1)} %bitcast.3) | data formatting | bytes 1048576
Async XLA Ops:
  1.5 1.6 %copy-start.1 = (bf16[2,2048,256]{2,1,0:T(8,128)(2,1)S(1)}, bf16[2,2048,256]{2,1,0:T(8,128)(2,1)}, u32[]{:S(2)}) copy-start(bf16[2,2048,256]{2,1,0:T(8,128)(2,1)} %modes_ref.1) | copy-start | bytes 6291460
  3.1 1.6 %copy-start.2 = (bf16[2,32,128,128]{3,2,1,0:T(8,128)(2,1)S(1)}, bf16[2,32,128,128]{3,2,1,0:T(8,128)(2,1)}, u32[]{:S(2)}) copy-start(bf16[2,32,128,128]{3,2,1,0:T(8,128)(2,1)} %stiff_ref.1) | copy-start | bytes 6291460
  4.6 1.6 %copy-start.3 = (bf16[2,32,128,128]{3,2,1,0:T(8,128)(2,1)S(1)}, bf16[2,32,128,128]{3,2,1,0:T(8,128)(2,1)}, u32[]{:S(2)}) copy-start(bf16[2,32,128,128]{3,2,1,0:T(8,128)(2,1)} %mass_ref.1) | copy-start | bytes 6291460
  6.2 0.7 copy-start.5
  6.9 0.7 copy-start.6
  7.6 3.5 %copy-start = (bf16[3072,512]{1,0:T(8,128)(2,1)S(1)}, bf16[3072,512]{1,0:T(8,128)(2,1)}, u32[]{:S(2)}) copy-start(bf16[3072,512]{1,0:T(8,128)(2,1)} %basis_ref.1) | copy-start | bytes 9437188
  11.1 8.7 %copy-start.4 = (f32[8,512]{1,0:T(8,128)S(1)}, f32[8,512]{1,0:T(8,128)}, u32[]{:S(2)}) copy-start(f32[8,512]{1,0:T(8,128)} %scale_ref.1) | copy-start | bytes 49156

commit v2 on v1

--- a/solution.py
+++ b/solution.py
@@ -9,18 +9,37 @@
 
 COLB_DEV = 4
 GROUP = 4
-HALVES = 2
+HALVES = 4
 MESH = pl.DeviceIdType.MESH
 
 
-def coupling_kernel(rows_ref, cols_ref, live_ref, modes_ref, stiff_ref, mass_ref, out_ref, phi_t, acc):
+def coupling_kernel(
+    rows_hbm, cols_hbm, live_hbm, modes_ref, stiff_ref, mass_ref, out_ref,
+    phi_t, acc, rows_ref, cols_ref, live_ref, sems,
+):
     leaf = pl.program_id(0)
+    fetches = [
+        pltpu.make_async_copy(src, dst, sems.at[n])
+        for n, (src, dst) in enumerate(((rows_hbm, rows_ref), (cols_hbm, cols_ref), (live_hbm, live_ref)))
+    ]
+
+    @pl.when(leaf == 0)
+    def _():
+        for fetch in fetches:
+            fetch.start()
+
     slots, block = stiff_ref.shape[1], stiff_ref.shape[2]
     rowb = modes_ref.shape[1] // block
     half = modes_ref.shape[2] // HALVES
     for r in range(rowb):
         phi_t[r] = modes_ref[0, r * block : (r + 1) * block, :].T
     acc[...] = jnp.zeros_like(acc)
+
+    @pl.when(leaf == 0)
+    def _():
+        for fetch in fetches:
+            fetch.wait()
+
     live = live_ref[leaf, 0]
 
     def step(g, carry):
@@ -51,21 +70,24 @@
     return pl.pallas_call(
         coupling_kernel,
         out_shape=jax.ShapeDtypeStruct((2 * HALVES, leaves, half, COLB_DEV * block), jnp.bfloat16),
-        grid_spec=pltpu.PrefetchScalarGridSpec(
-            num_scalar_prefetch=3,
+        grid_spec=pl.GridSpec(
             grid=(leaves,),
-            in_specs=[
-                pl.BlockSpec((1, ni, nmodes), lambda l, *_: (l, 0, 0)),
-                pl.BlockSpec((1, slots, block, block), lambda l, *_: (l, 0, 0, 0)),
-                pl.BlockSpec((1, slots, block, block), lambda l, *_: (l, 0, 0, 0)),
+            in_specs=[pl.BlockSpec(memory_space=pl.ANY)] * 3 + [
+                pl.BlockSpec((1, ni, nmodes), lambda l: (l, 0, 0)),
+                pl.BlockSpec((1, slots, block, block), lambda l: (l, 0, 0, 0)),
+                pl.BlockSpec((1, slots, block, block), lambda l: (l, 0, 0, 0)),
             ],
-            out_specs=pl.BlockSpec((2 * HALVES, 1, half, COLB_DEV * block), lambda l, *_: (0, l, 0, 0)),
+            out_specs=pl.BlockSpec((2 * HALVES, 1, half, COLB_DEV * block), lambda l: (0, l, 0, 0)),
             scratch_shapes=[
                 pltpu.VMEM((ni // block, nmodes, block), jnp.bfloat16),
                 pltpu.VMEM((COLB_DEV + 1, nmodes, 2 * block), jnp.float32),
+                pltpu.SMEM(row_index.shape, jnp.int32),
+                pltpu.SMEM(col_index.shape, jnp.int32),
+                pltpu.SMEM(live_blocks.shape, jnp.int32),
+                pltpu.SemaphoreType.DMA((3,)),
             ],
         ),
-        compiler_params=pltpu.CompilerParams(vmem_limit_bytes=40 << 20),
+        compiler_params=pltpu.CompilerParams(vmem_limit_bytes=62 << 20),
         name="leaf_couplings",
     )(row_index, col_index, live_blocks, modes, stiff, mass)
 
@@ -73,64 +95,21 @@
 UNROLL = 32
 
 
-def rows_kernel(dof_ref, basis_ref, out_ref, table, picked):
-    step = pl.program_id(0)
-    np_, cols = basis_ref.shape
-    nb = cols // 128
-    count = out_ref.shape[0]
-
-    @pl.when(step == 0)
-    def _():
-        for c in range(nb):
-            table[pl.ds(c, np_, nb), :] = basis_ref[:, c * 128 : (c + 1) * 128].astype(jnp.float32)
-
-    def body(i, carry):
-        for u in range(UNROLL):
-            t = i * UNROLL + u
-            which = dof_ref[step * count + t]
-            picked[pl.ds(t * nb, nb), :] = table[pl.ds(which * nb, nb), :]
-        return carry
-
-    lax.fori_loop(0, count // UNROLL, body, 0)
-    for c in range(nb):
-        out_ref[:, c * 128 : (c + 1) * 128] = picked[pl.ds(c, count, nb), :].astype(out_ref.dtype)
-
-
-def basis_rows(dof_list, basis):
-    total = dof_list.shape[0] * dof_list.shape[1]
-    np_, cols = basis.shape
-    count = 512
-    return pl.pallas_call(
-        rows_kernel,
-        out_shape=jax.ShapeDtypeStruct((total, cols), jnp.bfloat16),
-        grid_spec=pltpu.PrefetchScalarGridSpec(
-            num_scalar_prefetch=1,
-            grid=(total // count,),
-            in_specs=[pl.BlockSpec((np_, cols), lambda i, *_: (0, 0))],
-            out_specs=pl.BlockSpec((count, cols), lambda i, *_: (i, 0)),
-            scratch_shapes=[
-                pltpu.VMEM((np_ * cols // 128, 128), jnp.float32),
-                pltpu.VMEM((count * cols // 128, 128), jnp.float32),
-            ],
-        ),
-        compiler_params=pltpu.CompilerParams(vmem_limit_bytes=40 << 20),
-        name="basis_rows",
-    )(dof_list.reshape(total), basis)
-
-
 def flipped(index, bit):
     return index + (1 << bit) * (1 - 2 * ((index // (1 << bit)) % 2))
 
 
 def merge_kernel(
-    levels, c_ref, rows_hbm, scale_ref, out_ref,
-    rows, got, node0, part, node, total, sends, merged, t_send, t_got,
-    rows_sem, y_send, y_recv, core_send, core_recv, fwd_send, fwd_recv, lev_send, lev_recv, t_ssem, t_rsem,
+    levels, c_ref, dof_hbm, basis_hbm, scale_ref, out_ref,
+    dof_ref, basis, table, picked, rows, got, node0, part, node, total, sends, merged, t_send, t_got,
+    dof_sem, basis_sem, y_send, y_recv, core_send, core_recv, fwd_send, fwd_recv, lev_send, lev_recv, t_ssem, t_rsem,
 ):
     q, b = lax.axis_index("sub"), lax.axis_index("blk")
     chunks, leaves, depth, width = c_ref.shape
-    rows_copy = pltpu.make_async_copy(rows_hbm, rows, rows_sem)
-    rows_copy.start()
+    dof_copy = pltpu.make_async_copy(dof_hbm, dof_ref, dof_sem)
+    basis_copy = pltpu.make_async_copy(basis_hbm, basis, basis_sem)
+    dof_copy.start()
+    basis_copy.start()
     near, far = (q, flipped(b, 0)), (q, flipped(b, 1))
     peers = [(flipped(q, k), b) for k in range(levels)]
     barrier = pltpu.get_barrier_semaphore()
@@ -153,7 +132,24 @@
     t_copies = [remote(t_send.at[i], t_got.at[i], t_ssem.at[i], t_rsem.at[i], peers[0]) for i in range(chunks)]
     for copy in far_copies + near_copies:
         copy.start()
-    rows_copy.wait()
+    dof_copy.wait()
+    basis_copy.wait()
+    np_, cols = basis.shape
+    nb = cols // 128
+    count = dof_ref.shape[1]
+    for c in range(nb):
+        table[pl.ds(c, np_, nb), :] = basis[:, c * 128 : (c + 1) * 128].astype(jnp.float32)
+    for leaf in range(leaves):
+
+        def pick(i, carry, leaf=leaf):
+            for u in range(UNROLL):
+                which = dof_ref[leaf, i * UNROLL + u]
+                picked[pl.ds((i * UNROLL + u) * nb, nb), :] = table[pl.ds(which * nb, nb), :]
+            return carry
+
+        lax.fori_loop(0, count // UNROLL, pick, 0)
+        for c in range(nb):
+            rows[pl.ds(leaf * count, count), c * 128 : (c + 1) * 128] = picked[pl.ds(c, count, nb), :].astype(rows.dtype)
 
     def product(tile, which):
         res = None
@@ -166,10 +162,17 @@
     half = depth // 2
     own = q % 2
     for i in range(chunks):
-        part[i] = product(c_ref.at[i], b)
-    for i in range(chunks):
         near_copies[i].wait_recv()
-        part[i] += product(got.at[0, i], near[1])
+    batch = chunks // 2
+    for g in range(2):
+        res = None
+        for leaf in range(leaves):
+            for ref, which in ((c_ref, b), (got.at[0], near[1])):
+                tile = ref[pl.ds(g * batch, batch), leaf].reshape(batch * depth, width)
+                start = pl.multiple_of((leaf * 4 + which) * width, width)
+                one = jnp.dot(tile, rows[pl.ds(start, width), :], preferred_element_type=jnp.float32)
+                res = one if res is None else res + one
+        part[pl.ds(g * batch, batch)] = res.reshape(batch, depth, cols)
 
     def leaf_stage(i):
         far_copies[i].wait_recv()
@@ -211,9 +214,10 @@
         copy.wait_send()
 
 
-def merged_tree(coupling, rows, level_scale, levels):
+def merged_tree(coupling, dof_list, basis, level_scale, levels):
     chunks, leaves, depth, width = coupling.shape
-    cols = rows.shape[1]
+    np_, cols = basis.shape
+    nf = dof_list.shape[1]
     half = depth // 2
     bf, f32 = jnp.bfloat16, jnp.float32
     dma = pltpu.SemaphoreType.DMA
@@ -221,10 +225,14 @@
     return pl.pallas_call(
         functools.partial(merge_kernel, levels),
         out_shape=jax.ShapeDtypeStruct((chunks, 2, half, cols), bf),
-        in_specs=[vmem, pl.BlockSpec(memory_space=pl.ANY), vmem],
+        in_specs=[vmem] + [pl.BlockSpec(memory_space=pl.ANY)] * 2 + [vmem],
         out_specs=vmem,
         scratch_shapes=[
-            pltpu.VMEM(rows.shape, bf),
+            pltpu.SMEM(dof_list.shape, jnp.int32),
+            pltpu.VMEM(basis.shape, bf),
+            pltpu.VMEM((np_ * cols // 128, 128), f32),
+            pltpu.VMEM((nf * cols // 128, 128), f32),
+            pltpu.VMEM((leaves * nf, cols), bf),
             pltpu.VMEM((3, chunks, leaves, depth, width), bf),
             pltpu.VMEM((chunks, 2, half, cols), f32),
             pltpu.VMEM((chunks, depth, cols), f32),
@@ -234,7 +242,7 @@
             pltpu.VMEM((levels, chunks, half, cols), bf),
             pltpu.VMEM((chunks, half, cols), bf),
             pltpu.VMEM((chunks, half, cols), bf),
-            dma,
+            dma, dma,
             dma((chunks,)), dma((chunks,)), dma((chunks,)), dma((chunks,)), dma((chunks,)), dma((chunks,)),
             dma((levels, chunks)), dma((levels, chunks)), dma((chunks,)), dma((chunks,)),
         ],
@@ -242,7 +250,7 @@
             collective_id=0, has_side_effects=True, vmem_limit_bytes=40 << 20
         ),
         name="merged_tree",
-    )(coupling, rows, level_scale)
+    )(coupling, dof_list, basis, level_scale)
 
 
 def per_device(
@@ -258,8 +266,7 @@
 ):
     levels = lax.axis_size("sub").bit_length() - 1
     coupling = leaf_couplings(row_index, col_index, live_blocks, modes, stiff_blocks, mass_blocks)
-    rows = basis_rows(dof_list, parent_basis)
-    out = merged_tree(coupling, rows, level_scale, levels)
+    out = merged_tree(coupling, dof_list, parent_basis, level_scale, levels)
     return out.reshape(1, 2, modes.shape[2], parent_basis.shape[1])
 
 

time: 69.2 us -> 63.5 us (0.918); the launches traced: 69.8 us -> 63.3 us
  Pallas kernels: 61.4 us -> 58.1 us
  local copies, waits for them, and re-layouts: 8.39 us -> 5.21 us
    pallas_call x1 -> x0, Pallas kernels: 8.69 us -> none  [basis_rows(): pl.pallas_call(rows_kernel, out_shape=jax.ShapeDtypeStruct((total, cols),...]
    unnamed x17 -> x10, local copies, waits for them, and re-layouts: 8.39 us -> 5.21 us
    pallas_call x1, Pallas kernels: 3.45 us -> 6.22 us  [leaf_couplings(): pl.pallas_call(coupling_kernel, out_shape=jax.ShapeDtypeStruct((2 * HALVE...]
    pallas_call x1, Pallas kernels: 49.2 us -> 51.8 us  [merged_tree(): pl.pallas_call(functools.partial(merge_kernel, levels), out_shape=jax.Sha...]
where the time goes in v2:
time: 63.5 us; the launch traced here: 63.3 us
  Pallas kernels  58.1 us (91%)
  local copies, waits for them, and re-layouts  5.21 us (8%)
    pallas_call x1, Pallas kernels, merged_tree(): pl.pallas_call(functools.partial(merge_kernel, levels), out_shape=jax.Sha...  51.8 us
    pallas_call x1, Pallas kernels, leaf_couplings(): pl.pallas_call(coupling_kernel, out_shape=jax.ShapeDtypeStruct((2 * HALVE...  6.22 us
    unnamed x10, local copies, waits for them, and re-layouts  5.21 us

profile of v2, /device:TPU:0, one launch (start us, length us, event | category | flops | bytes accessed | tf_op | source)
XLA Modules:
  0.0 63.3 jit_solution(917097504626442108)
XLA Ops:
  0.0 1.3 %copy.10.live_hbm = s32[2,1]{1,0:T(2,128)} copy(s32[2,1]{0,1:T(1,128)} %param.14) | data formatting | bytes 16 | tf_op args[5]
  1.3 0.0 copy-start.2
  1.3 0.0 copy-start.3
  1.3 6.2 %leaf_couplings.1.c_ref = bf16[8,2,64,512]{3,2,1,0:T(8,128)(2,1)} custom-call(s32[2,32]{1,0:T(2,128)} %rows_hbm.1, s32[2,32]{1,0:T(2,128)} %cols_hbm.1, s32[2,1]{1,0:T(2,128)} %copy.10.live_hbm, bf16[2,2048,256]{2,1,0:T(8,128)(2,1)} %modes_ref.1, bf16[2,32,128,128]{3,2,1,0:T(8,128)(2,1)} %stiff_ref.1, bf16[2,32,128,128]{3,2,1,0:T(8,128)(2,1)} %mass_ref.1), custom_call_target="tpu_custom_call" | custom-call | tf_op jit(solution)/shard_map/leaf_couplings/pallas_call | solution.py:70
  7.5 0.0 copy-done.2
  7.5 0.0 copy-done.3
  7.5 0.0 copy-start
  7.6 1.2 %copy-done = bf16[8,2,64,512]{3,2,1,0:T(8,128)(2,1)S(1)} copy-done((bf16[8,2,64,512]{3,2,1,0:T(8,128)(2,1)S(1)}, bf16[8,2,64,512]{3,2,1,0:T(8,128)(2,1)}, u32[]{:S(2)}) %copy-start) | copy-done | bytes 1048600
  8.8 0.0 copy-start.1
  8.8 1.9 %copy-done.1 = bf16[3072,512]{1,0:T(8,128)(2,1)S(1)} copy-done((bf16[3072,512]{1,0:T(8,128)(2,1)S(1)}, bf16[3072,512]{1,0:T(8,128)(2,1)}, u32[]{:S(2)}) %copy-start.1) | copy-done | bytes 3145752
  10.7 51.8 %merged_tree.1 = bf16[8,2,32,512]{3,2,1,0:T(8,128)(2,1)S(1)} custom-call(bf16[8,2,64,512]{3,2,1,0:T(8,128)(2,1)S(1)} %copy-done, s32[2,2048]{1,0:T(2,128)S(1)} %copy-done.2, bf16[3072,512]{1,0:T(8,128)(2,1)S(1)} %copy-done.1, f32[8,512]{1,0:T(8,128)S(1)} %copy-done.3), custom_call_target="tpu_custom_call" | custom-call | tf_op jit(solution)/shard_map/merged_tree/pallas_call | solution.py:225
  62.5 0.8 %copy.12 = bf16[1,2,256,512]{3,2,1,0:T(8,128)(2,1)} copy(bf16[1,2,256,512]{3,2,1,0:T(8,128)(2,1)S(1)} %bitcast.1) | data formatting | bytes 1048576
Async XLA Ops:
  1.3 6.2 %copy-start.2 = (s32[2,2048]{1,0:T(2,128)S(1)}, s32[2,2048]{1,0:T(2,128)}, u32[]{:S(2)}) copy-start(s32[2,2048]{1,0:T(2,128)} %dof_hbm.1) | copy-start | bytes 49156
  1.3 6.2 %copy-start.3 = (f32[8,512]{1,0:T(8,128)S(1)}, f32[8,512]{1,0:T(8,128)}, u32[]{:S(2)}) copy-start(f32[8,512]{1,0:T(8,128)} %scale_ref.1) | copy-start | bytes 49156
  7.5 1.2 %copy-start = (bf16[8,2,64,512]{3,2,1,0:T(8,128)(2,1)S(1)}, bf16[8,2,64,512]{3,2,1,0:T(8,128)(2,1)}, u32[]{:S(2)}) copy-start(bf16[8,2,64,512]{3,2,1,0:T(8,128)(2,1)} %leaf_couplings.1.c_ref) | copy-start | bytes 3145732
  8.8 1.9 %copy-start.1 = (bf16[3072,512]{1,0:T(8,128)(2,1)S(1)}, bf16[3072,512]{1,0:T(8,128)(2,1)}, u32[]{:S(2)}) copy-start(bf16[3072,512]{1,0:T(8,128)(2,1)} %basis_hbm.1) | copy-start | bytes 9437188

commit v3 on v2

--- a/solution.py
+++ b/solution.py
@@ -9,7 +9,7 @@
 
 COLB_DEV = 4
 GROUP = 4
-HALVES = 4
+HALVES = 2
 MESH = pl.DeviceIdType.MESH
 
 
@@ -40,7 +40,7 @@
         for fetch in fetches:
             fetch.wait()
 
-    live = live_ref[leaf, 0]
+    live = live_ref[0, leaf]
 
     def step(g, carry):
         prods = []
@@ -100,15 +100,17 @@
 
 
 def merge_kernel(
-    levels, c_ref, dof_hbm, basis_hbm, scale_ref, out_ref,
-    dof_ref, basis, table, picked, rows, got, node0, part, node, total, sends, merged, t_send, t_got,
-    dof_sem, basis_sem, y_send, y_recv, core_send, core_recv, fwd_send, fwd_recv, lev_send, lev_recv, t_ssem, t_rsem,
+    levels, c_hbm, dof_hbm, basis_hbm, scale_ref, out_ref,
+    c_ref, dof_ref, basis, table, picked, rows, got, node0, part, node, total, sends, merged, t_send, t_got,
+    c_sem, dof_sem, basis_sem, y_send, y_recv, core_send, core_recv, fwd_send, fwd_recv, lev_send, lev_recv, t_ssem, t_rsem,
 ):
     q, b = lax.axis_index("sub"), lax.axis_index("blk")
-    chunks, leaves, depth, width = c_ref.shape
+    chunks, leaves, depth, width = c_hbm.shape
+    c_copy = pltpu.make_async_copy(c_hbm, c_ref, c_sem)
     dof_copy = pltpu.make_async_copy(dof_hbm, dof_ref, dof_sem)
     basis_copy = pltpu.make_async_copy(basis_hbm, basis, basis_sem)
     dof_copy.start()
+    c_copy.start()
     basis_copy.start()
     near, far = (q, flipped(b, 0)), (q, flipped(b, 1))
     peers = [(flipped(q, k), b) for k in range(levels)]
@@ -122,8 +124,8 @@
             src_ref=src, dst_ref=dst, send_sem=ssem, recv_sem=rsem, device_id=peer, device_id_type=MESH
         )
 
-    far_copies = [remote(c_ref.at[i], got.at[1, i], y_send.at[i], y_recv.at[i], far) for i in range(chunks)]
-    near_copies = [remote(c_ref.at[i], got.at[0, i], core_send.at[i], core_recv.at[i], near) for i in range(chunks)]
+    far_copies = [remote(c_hbm.at[i], got.at[1, i], y_send.at[i], y_recv.at[i], far) for i in range(chunks)]
+    near_copies = [remote(c_hbm.at[i], got.at[0, i], core_send.at[i], core_recv.at[i], near) for i in range(chunks)]
     fwd_copies = [remote(got.at[1, i], got.at[2, i], fwd_send.at[i], fwd_recv.at[i], near) for i in range(chunks)]
     lev_copies = [
         [remote(sends.at[k, i], merged.at[k, i], lev_send.at[k, i], lev_recv.at[k, i], peers[k]) for i in range(chunks)]
@@ -133,6 +135,7 @@
     for copy in far_copies + near_copies:
         copy.start()
     dof_copy.wait()
+    c_copy.wait()
     basis_copy.wait()
     np_, cols = basis.shape
     nb = cols // 128
@@ -206,10 +209,10 @@
         out_ref[i, 1 - own] = (node0[i, 1 - own] + t_got[i].astype(jnp.float32)).astype(out_ref.dtype)
 
     stages = [leaf_stage] + [functools.partial(level_stage, k) for k in range(1, levels + 1)] + [last_stage]
-    for t in range(chunks + len(stages) - 1):
+    for t in range(2 * (chunks - 1) + len(stages)):
         for s, stage in enumerate(stages):
-            if 0 <= t - s < chunks:
-                stage(t - s)
+            if (t - s) % 2 == 0 and 0 <= t - s < 2 * chunks:
+                stage((t - s) // 2)
     for copy in far_copies + near_copies + fwd_copies + [c for row in lev_copies for c in row] + t_copies:
         copy.wait_send()
 
@@ -225,9 +228,10 @@
     return pl.pallas_call(
         functools.partial(merge_kernel, levels),
         out_shape=jax.ShapeDtypeStruct((chunks, 2, half, cols), bf),
-        in_specs=[vmem] + [pl.BlockSpec(memory_space=pl.ANY)] * 2 + [vmem],
+        in_specs=[pl.BlockSpec(memory_space=pl.ANY)] * 3 + [vmem],
         out_specs=vmem,
         scratch_shapes=[
+            pltpu.VMEM(coupling.shape, bf),
             pltpu.SMEM(dof_list.shape, jnp.int32),
             pltpu.VMEM(basis.shape, bf),
             pltpu.VMEM((np_ * cols // 128, 128), f32),
@@ -242,12 +246,12 @@
             pltpu.VMEM((levels, chunks, half, cols), bf),
             pltpu.VMEM((chunks, half, cols), bf),
             pltpu.VMEM((chunks, half, cols), bf),
-            dma, dma,
+            dma, dma, dma,
             dma((chunks,)), dma((chunks,)), dma((chunks,)), dma((chunks,)), dma((chunks,)), dma((chunks,)),
             dma((levels, chunks)), dma((levels, chunks)), dma((chunks,)), dma((chunks,)),
         ],
         compiler_params=pltpu.CompilerParams(
-            collective_id=0, has_side_effects=True, vmem_limit_bytes=40 << 20
+            collective_id=0, has_side_effects=True, vmem_limit_bytes=62 << 20
         ),
         name="merged_tree",
     )(coupling, dof_list, basis, level_scale)
@@ -265,7 +269,7 @@
     level_scale,
 ):
     levels = lax.axis_size("sub").bit_length() - 1
-    coupling = leaf_couplings(row_index, col_index, live_blocks, modes, stiff_blocks, mass_blocks)
+    coupling = leaf_couplings(row_index, col_index, live_blocks.T, modes, stiff_blocks, mass_blocks)
     out = merged_tree(coupling, dof_list, parent_basis, level_scale, levels)
     return out.reshape(1, 2, modes.shape[2], parent_basis.shape[1])
 

time: 63.5 us -> 63 us (level)
  local copies, waits for them, and re-layouts: 5.21 us -> 1.87 us
  Pallas kernels: 58.1 us -> 60.5 us
    unnamed x10 -> x1, local copies, waits for them, and re-layouts: 5.21 us -> 1.87 us
    pallas_call x1, Pallas kernels: 51.8 us -> 54.9 us  [merged_tree(): pl.pallas_call(functools.partial(merge_kernel, levels), out_shape=jax.Sha...]
where the time goes in v3:
time: 63 us; the launch traced here: 62.4 us
  Pallas kernels  60.5 us (96%)
  local copies, waits for them, and re-layouts  1.87 us (3%)
    pallas_call x1, Pallas kernels, merged_tree(): pl.pallas_call(functools.partial(merge_kernel, levels), out_shape=jax.Sha...  54.9 us
    pallas_call x1, Pallas kernels, leaf_couplings(): pl.pallas_call(coupling_kernel, out_shape=jax.ShapeDtypeStruct((2 * HALVE...  5.62 us
    unnamed x1, local copies, waits for them, and re-layouts  1.87 us

profile of v3, /device:TPU:0, one launch (start us, length us, event | category | flops | bytes accessed | tf_op | source)
XLA Modules:
  0.0 62.4 jit_solution(13290261357010962441)
XLA Ops:
  0.0 5.6 %leaf_couplings.1.c_hbm = bf16[4,2,128,512]{3,2,1,0:T(8,128)(2,1)} custom-call(s32[2,32]{1,0:T(2,128)} %rows_hbm.1, s32[2,32]{1,0:T(2,128)} %cols_hbm.1, s32[1,2]{1,0:T(1,128)} %bitcast.3, bf16[2,2048,256]{2,1,0:T(8,128)(2,1)} %modes_ref.1, bf16[2,32,128,128]{3,2,1,0:T(8,128)(2,1)} %stiff_ref.1, bf16[2,32,128,128]{3,2,1,0:T(8,128)(2,1)} %mass_ref.1), custom_call_target="tpu_custom_call" | custom-call | tf_op jit(solution)/shard_map/leaf_couplings/pallas_call | solution.py:70
  5.6 54.9 %merged_tree.1 = bf16[4,2,64,512]{3,2,1,0:T(8,128)(2,1)} custom-call(bf16[4,2,128,512]{3,2,1,0:T(8,128)(2,1)} %leaf_couplings.1.c_hbm, s32[2,2048]{1,0:T(2,128)} %dof_hbm.1, bf16[3072,512]{1,0:T(8,128)(2,1)} %basis_hbm.1, f32[8,512]{1,0:T(8,128)} %scale_ref.1), custom_call_target="tpu_custom_call" | custom-call | tf_op jit(solution)/shard_map/merged_tree/pallas_call | solution.py:228
  60.5 1.9 %copy.11 = bf16[1,2,256,512]{3,2,1,0:T(8,128)(2,1)} copy(bf16[1,2,256,512]{3,2,1,0:T(8,128)(2,1)} %bitcast.2) | data formatting | bytes 1048576

commit v4 on v3

--- a/solution.py
+++ b/solution.py
@@ -132,7 +132,8 @@
         for k in range(levels)
     ]
     t_copies = [remote(t_send.at[i], t_got.at[i], t_ssem.at[i], t_rsem.at[i], peers[0]) for i in range(chunks)]
-    for copy in far_copies + near_copies:
+    early = chunks // 2
+    for copy in far_copies[:early] + near_copies:
         copy.start()
     dof_copy.wait()
     c_copy.wait()
@@ -162,6 +163,10 @@
             res = one if res is None else res + one
         return res
 
+    for copy in far_copies[:early]:
+        copy.wait_send()
+    for copy in far_copies[early:]:
+        copy.start()
     half = depth // 2
     own = q % 2
     for i in range(chunks):
@@ -213,7 +218,7 @@
         for s, stage in enumerate(stages):
             if (t - s) % 2 == 0 and 0 <= t - s < 2 * chunks:
                 stage((t - s) // 2)
-    for copy in far_copies + near_copies + fwd_copies + [c for row in lev_copies for c in row] + t_copies:
+    for copy in far_copies[early:] + near_copies + fwd_copies + [c for row in lev_copies for c in row] + t_copies:
         copy.wait_send()
 
 

time: 63 us -> 64.7 us (1.027); the launches traced: 62.4 us -> 65.8 us
  Pallas kernels: 60.5 us -> 63.9 us
    pallas_call x1, Pallas kernels: 54.9 us -> 56.7 us  [merged_tree(): pl.pallas_call(functools.partial(merge_kernel, levels), out_shape=jax.Sha...]
    pallas_call x1, Pallas kernels: 5.62 us -> 7.15 us  [leaf_couplings(): pl.pallas_call(coupling_kernel, out_shape=jax.ShapeDtypeStruct((2 * HALVE...]
where the time goes in v4:
time: 64.7 us; the launch traced here: 65.8 us
  Pallas kernels  63.9 us (99%)
  local copies, waits for them, and re-layouts  1.87 us (3%)
    pallas_call x1, Pallas kernels, merged_tree(): pl.pallas_call(functools.partial(merge_kernel, levels), out_shape=jax.Sha...  56.7 us
    pallas_call x1, Pallas kernels, leaf_couplings(): pl.pallas_call(coupling_kernel, out_shape=jax.ShapeDtypeStruct((2 * HALVE...  7.15 us
    unnamed x1, local copies, waits for them, and re-layouts  1.87 us

profile of v4, /device:TPU:0, one launch (start us, length us, event | category | flops | bytes accessed | tf_op | source)
XLA Modules:
  0.0 65.8 jit_solution(17675431212007876436)
XLA Ops:
  0.0 7.1 %leaf_couplings.1.c_hbm = bf16[4,2,128,512]{3,2,1,0:T(8,128)(2,1)} custom-call(s32[2,32]{1,0:T(2,128)} %rows_hbm.1, s32[2,32]{1,0:T(2,128)} %cols_hbm.1, s32[1,2]{1,0:T(1,128)} %bitcast.3, bf16[2,2048,256]{2,1,0:T(8,128)(2,1)} %modes_ref.1, bf16[2,32,128,128]{3,2,1,0:T(8,128)(2,1)} %stiff_ref.1, bf16[2,32,128,128]{3,2,1,0:T(8,128)(2,1)} %mass_ref.1), custom_call_target="tpu_custom_call" | custom-call | tf_op jit(solution)/shard_map/leaf_couplings/pallas_call | solution.py:70
  7.2 56.7 %merged_tree.1 = bf16[4,2,64,512]{3,2,1,0:T(8,128)(2,1)} custom-call(bf16[4,2,128,512]{3,2,1,0:T(8,128)(2,1)} %leaf_couplings.1.c_hbm, s32[2,2048]{1,0:T(2,128)} %dof_hbm.1, bf16[3072,512]{1,0:T(8,128)(2,1)} %basis_hbm.1, f32[8,512]{1,0:T(8,128)} %scale_ref.1), custom_call_target="tpu_custom_call" | custom-call | tf_op jit(solution)/shard_map/merged_tree/pallas_call | solution.py:233
  63.9 1.9 %copy.11 = bf16[1,2,256,512]{3,2,1,0:T(8,128)(2,1)} copy(bf16[1,2,256,512]{3,2,1,0:T(8,128)(2,1)} %bitcast.2) | data formatting | bytes 1048576
